TPU v7x, 512 devices: a whole 4x4x16 slice. The times are simulated.
512 devices in a mesh: blk: 16 (over y, x_hi, core), grp: 32 (over z, x_lo).
Axes of the slice: x: 4 (x_hi: 2, x_lo: 2; x = x_hi * 2 + x_lo), y: 4, z: 16, core: 2. Of those that a mesh axis runs over, the one named last changes fastest.
Arguments:
- factor: bfloat16 [8192, 8192], P('grp', 'blk'), may hold values from -1 to 108
- scales: float32 [64, 64], P('grp', 'blk'), may hold values from 0.5 to 2
- basis_block: bfloat16 [8192, 8192], P('grp', 'blk'), may hold values from -6 to 6
Outputs:
- new_basis: float32 [8192, 8192], P('grp', 'blk')
All inputs are finite; a program needn't handle non-finite values.
Results may differ from a plain program's by a relative error of at most 0.0029.
Values may be sent and summed in bfloat16 or wider, within the bound.
A program may use at most 64 MiB of HBM per device.

v0:
```python
import jax
import jax.numpy as jnp
from jax import lax
from jax.sharding import PartitionSpec as P

M = 8192


def dequantize(quantized, scale_block):
    row_groups = scale_block.shape[0]
    col_groups = scale_block.shape[1]
    width = quantized.shape[0] // row_groups
    shaped = quantized.astype(jnp.float32).reshape(row_groups, width, col_groups, width)
    return (shaped * scale_block[:, None, :, None]).reshape(quantized.shape).astype(jnp.bfloat16)


def per_device(factor, scales, basis_block):
    block_cols = basis_block.shape[1]
    dequant = dequantize(factor, scales)
    gathered = lax.all_gather(basis_block, "grp", axis=0, tiled=True)
    product_rows = jnp.dot(
        lax.all_gather(dequant, "blk", axis=1, tiled=True),
        gathered,
        preferred_element_type=jnp.float32,
    )
    gram_local = jnp.dot(product_rows.T, product_rows, precision=lax.Precision.HIGHEST)
    gram_total = lax.psum(gram_local, "grp")
    gram_mean = gram_total / M
    lower_tri = jnp.linalg.cholesky(gram_mean)
    inverse = jax.scipy.linalg.solve_triangular(
        lower_tri, jnp.eye(block_cols, dtype=jnp.float32), lower=True
    )
    return jnp.dot(product_rows, inverse.T, precision=lax.Precision.HIGHEST)


def solution(mesh):
    return jax.shard_map(
        per_device,
        mesh=mesh,
        in_specs=(P("grp", "blk"), P("grp", "blk"), P("grp", "blk")),
        out_specs=P("grp", "blk"),
        check_vma=False,
    )
```

profile of v0, /device:TPU:16, one launch (start us, length us, event | category | flops | bytes accessed | tf_op | source)
XLA Modules:
  0.0 708.0 jit_solution(13088897053693757330)
XLA Ops:
  6.5 0.8 mul.11
  7.4 1.7 fusion.14
  9.2 0.7 all-gather.5.cloned.1.call-update
  9.9 75.4 %all-gather.3.cloned.1.call-done = bf16[256,8192]{1,0:T(8,128)(2,1)} async-done(((bf16[256,512]{1,0:T(8,128)(2,1)}), bf16[256,8192]{1,0:T(8,128)(2,1)}) %all-gather.3.cloned.1.call-update) | async-done | bytes 4194320 | tf_op jit(solution)/shard_map/all_gather | solution.py:22
  85.3 197.9 %all-gather.5.cloned.1.call-done = bf16[8192,512]{1,0:T(8,128)(2,1)} async-done(((bf16[256,512]{1,0:T(8,128)(2,1)}), bf16[8192,512]{1,0:T(8,128)(2,1)}) %all-gather.5.cloned.1.call-update) | async-done | bytes 8388624 | tf_op jit(solution)/shard_map/all_gather | solution.py:20
  283.1 7.0 fusion.42
  290.1 0.8 copy-done
  290.9 2.1 fusion.43
  293.0 0.8 iota_compare_fusion
  293.9 263.4 %all-reduce.3.cloned.1.call-done = f32[512,512]{0,1:T(8,128)} async-done(((f32[512,512]{0,1:T(8,128)}), f32[512,512]{0,1:T(8,128)}) %all-reduce.3.cloned.1.call-update) | async-done | bytes 1048592 | tf_op jit(solution)/shard_map/psum | solution.py:27
  557.3 1.3 broadcast_multiply_fusion
  558.7 0.3 copy.5
  559.0 1.5 fusion.8
  560.5 11.7 %cholesky.104 = f32[128,128]{1,0:T(8,128)S(1)} custom-call(f32[128,128]{1,0:T(8,128)S(1)} %cholesky.266), custom_call_target="Cholesky" | custom-call | tf_op jit(solution)/shard_map/jit(cholesky)/cholesky | solution.py:29
  572.2 9.8 %custom-call.31 = f32[1,128,128]{1,2,0:T(8,128)S(1)} custom-call(f32[1,128,128]{2,1,0:T(8,128)S(1)} %get-tuple-element.32), custom_call_target="InvertDiagBlocksLowerTriangular" | custom-call | tf_op jit(solution)/shard_map/jit(cholesky)/cholesky | solution.py:29
  582.2 0.3 constant_dynamic-update-slice_fusion.3
  582.5 0.3 convolution_subtract_fusion.3
  582.8 11.9 %cholesky.217 = f32[128,128]{1,0:T(8,128)S(1)} custom-call(f32[128,128]{1,0:T(8,128)S(1)} %cholesky.270), custom_call_target="Cholesky" | custom-call | tf_op jit(solution)/shard_map/jit(cholesky)/cholesky | solution.py:29
  594.8 9.8 %custom-call.32 = f32[1,128,128]{1,2,0:T(8,128)S(1)} custom-call(f32[1,128,128]{2,1,0:T(8,128)S(1)} %get-tuple-element.29), custom_call_target="InvertDiagBlocksLowerTriangular" | custom-call | tf_op jit(solution)/shard_map/jit(cholesky)/cholesky | solution.py:29
  604.6 0.3 convolution_dynamic-update-slice_fusion
  604.9 0.4 convolution_subtract_fusion.4
  605.3 11.7 %cholesky.238 = f32[128,128]{1,0:T(8,128)S(1)} custom-call(f32[128,128]{1,0:T(8,128)S(1)} %cholesky.275), custom_call_target="Cholesky" | custom-call | tf_op jit(solution)/shard_map/jit(cholesky)/cholesky | solution.py:29
  617.0 0.7 compare_reduce_fusion.1
  617.7 9.8 %custom-call.33 = f32[1,128,128]{1,2,0:T(8,128)S(1)} custom-call(f32[1,128,128]{2,1,0:T(8,128)S(1)} %get-tuple-element.26), custom_call_target="InvertDiagBlocksLowerTriangular" | custom-call | tf_op jit(solution)/shard_map/jit(cholesky)/cholesky | solution.py:29
  627.5 0.2 convolution_dynamic-update-slice_fusion.1
  627.7 0.4 convolution_subtract_fusion.5
  628.1 11.9 %cholesky.255 = f32[128,128]{1,0:T(8,128)S(1)} custom-call(f32[128,128]{1,0:T(8,128)S(1)} %convolution_subtract_fusion.5), custom_call_target="Cholesky" | custom-call | tf_op jit(solution)/shard_map/jit(cholesky)/cholesky | solution.py:29
  640.1 0.6 compare_reduce_fusion
  640.7 0.7 compare_reduce_fusion.2
  644.0 0.1 select_select_fusion
  644.1 10.6 %while.1 = (s32[]{:T(128)}, f32[512,512]{1,0:T(8,128)S(1)}, s32[4,2]{0,1:T(2,128)S(1)}, f32[4,128,128]{2,1,0:T(8,128)}, s32[]{:T(128)}) while((s32[]{:T(128)}, f32[512,512]{1,0:T(8,128)S(1)}, s32[4,2]{0,1:T(2,128)S(1)}, f32[4,128,128]{2,1,0:T(8,128)}, s32[]{:T(128)}) %tuple.27), condition=%wide.while_cond, body=%wide.while_body.sunk | while | flops 2 | bytes 132705 | solution.py:30
  644.2 0.6 fusion.55
  644.8 2.0 bitcast_dynamic-update-slice_fusion.2
  646.8 0.6 fusion.55
  647.4 2.0 bitcast_dynamic-update-slice_fusion.2
  649.4 0.6 fusion.55
  650.0 2.0 bitcast_dynamic-update-slice_fusion.2
  652.1 0.6 fusion.55
  652.7 2.0 bitcast_dynamic-update-slice_fusion.2
  654.7 40.1 %custom-call.34 = f32[4,128,128]{1,2,0:T(8,128)S(1)} custom-call(f32[4,128,128]{2,1,0:T(8,128)} %get-tuple-element.12), custom_call_target="InvertDiagBlocksLowerTriangular" | custom-call | tf_op jit(solution)/shard_map/jit(_solve_triangular)/triangular_solve | solution.py:30
  694.8 1.1 fusion.20
  695.9 0.4 convolution_subtract_fusion.1
  696.2 0.4 fusion.32
  696.7 0.4 convolution_subtract_fusion
  697.1 0.4 fusion.30
  697.5 0.6 convolution_subtract_fusion.2
  698.2 0.4 fusion.29
  698.6 2.9 fusion
  (22 shorter events, 0.8 us)
Async XLA Ops:
  6.5 78.7 %all-gather.3.cloned.1.call-start = ((), (), s32[]{:S(2)}) async-start(), calls=%async_computation | async-start | bytes 4456448 | tf_op jit(solution)/shard_map/all_gather | solution.py:22
  9.1 274.0 %all-gather.5.cloned.1.call-start = ((), (), s32[]{:S(2)}) async-start(), calls=%async_computation.1 | async-start | bytes 8650752 | tf_op jit(solution)/shard_map/all_gather | solution.py:20
  9.9 547.5 %all-reduce.3.cloned.1.call-start = ((), (), s32[]{:S(2)}) async-start(), calls=%async_computation.2 | async-start | bytes 2097152 | tf_op jit(solution)/shard_map/psum | solution.py:27
  290.1 0.8 copy-start
Sparse Core Ops, SparseCore 0:
  10.6 74.6 all-gather.2
  87.3 195.7 all-gather.4
  293.1 264.1 all-reduce.2
where the time goes:
time: 709 us; the launch traced here: 708 us
  waiting for transfers between devices  537 us (76%)
  other arithmetic  124 us (17%)
  matrix products  17.6 us (2%)
  between operations  15.9 us (2%)
  local copies, waits for them, and re-layouts  12.6 us (2%)
    psum x1, waiting for transfers between devices, per_device(): gram_total = lax.psum(gram_local, 'grp')  263 us
    all_gather x1, waiting for transfers between devices, per_device(): gathered = lax.all_gather(basis_block, 'grp', axis=0, tiled=True)  198 us
    another operation x14, other arithmetic, per_device(): lower_tri = jnp.linalg.cholesky(gram_mean)  78.9 us
    all_gather x1, waiting for transfers between devices, per_device(): lax.all_gather(dequant, 'blk', axis=1, tiled=True)  75.4 us
    another operation x3, other arithmetic, per_device(): jax.scipy.linalg.solve_triangular(lower_tri, jnp.eye(block_cols, dtype=jn...  40.3 us
  transfers between devices with their start and end apart: 3, of which 3 were waited for; matrix products, arithmetic and copies ran while one was open for 0% of the time, Pallas kernels for 0%

commit v1 on v0

v1 whole, which is shorter than its diff:
```python
import functools

import jax
import jax.numpy as jnp
from jax import lax
from jax.experimental import pallas as pl
from jax.experimental.pallas import tpu as pltpu
from jax.sharding import PartitionSpec as P

M = 8192
NY, NX, NZ = 4, 4, 16
ROWS, COLS = 256, 512
HALF = ROWS // 2
TILE = 128
NT = COLS // TILE
PAIRS = [(i, j) for i in range(NT) for j in range(i + 1)]
PER_CORE = len(PAIRS) // 2
PIECE = TILE // NZ
SUB = 32
STEP = 4
HIGHEST = lax.Precision.HIGHEST


def dequantize(quantized, scale_block):
    row_groups, col_groups = scale_block.shape
    width = quantized.shape[0] // row_groups
    shaped = quantized.astype(jnp.float32).reshape(row_groups, width, col_groups, width)
    return (shaped * scale_block[:, None, :, None]).reshape(quantized.shape).astype(jnp.bfloat16)


def place():
    blk, grp = lax.axis_index("blk"), lax.axis_index("grp")
    core, x_hi, y = lax.rem(blk, 2), lax.rem(lax.div(blk, 2), 2), lax.div(blk, 4)
    z, x_lo = lax.div(grp, 2), lax.rem(grp, 2)
    return y, x_hi, x_lo, z, core


def device(y, x, z, core):
    return {"blk": (y * 2 + lax.div(x, 2)) * 2 + core, "grp": z * 2 + lax.rem(x, 2)}


def remote(src, dst, send, recv, to):
    return pltpu.make_async_remote_copy(
        src_ref=src, dst_ref=dst, send_sem=send, recv_sem=recv,
        device_id=to, device_id_type=pl.DeviceIdType.MESH,
    )


def gather_kernel(
    d_ref, b_ref, image_ref, gram_ref,
    d_xy, d_yx, basis, part, other, mine, arrived, total,
    own_sem, swap_s, swap_r, xy_s, xy_r, yx_s, yx_r, ring_s, ring_r, sib_s, sib_r,
    pair_s, pair_r, rs_s, rs_r, ag_s, ag_r,
):
    y, x_hi, x_lo, z, core = place()
    x = x_hi * 2 + x_lo
    sibling = device(y, x, z, 1 - core)
    partner_x = x_hi * 2 + core
    partner = device(y, partner_x, z, x_lo)
    moved = x_lo != core

    def x_peer(d):
        return device(y, lax.rem(x + d, NX), z, core)

    def y_peer(d):
        return device(lax.rem(y + d, NY), x, z, core)

    def z_peer(d):
        return device(y, x, lax.rem(z + d, NZ), core)

    barrier = pltpu.get_barrier_semaphore()

    def greet(to):
        pl.semaphore_signal(barrier, inc=1, device_id=to, device_id_type=pl.DeviceIdType.MESH)

    greet(sibling)
    for d in range(1, 4):
        greet(x_peer(d))
        greet(y_peer(d))

    @pl.loop(1, NZ)
    def _(d):
        greet(z_peer(d))

    @pl.when(moved)
    def _():
        greet(partner)
        pl.semaphore_wait(barrier, 23)

    @pl.when(jnp.logical_not(moved))
    def _():
        pl.semaphore_wait(barrier, 22)

    halves = [pl.ds(0, HALF), pl.ds(HALF, HALF)]

    @pl.when(moved)
    def _():
        sent = [
            remote(b_ref.at[halves[0]], basis.at[z, x_lo, 0], swap_s.at[0], swap_r.at[0], partner),
            remote(b_ref.at[halves[1]], basis.at[z, x_lo, 1], swap_s.at[1], swap_r.at[1], partner),
            remote(d_ref.at[halves[0]], d_xy.at[y, partner_x], swap_s.at[2], swap_r.at[2], partner),
            remote(d_ref.at[halves[1]], d_yx.at[partner_x, y], swap_s.at[3], swap_r.at[3], partner),
        ]
        for copy in sent:
            copy.start()
        for copy in sent:
            copy.wait()

    @pl.when(jnp.logical_not(moved))
    def _():
        kept = [
            pltpu.make_async_copy(b_ref.at[halves[0]], basis.at[z, core, 0], own_sem.at[0]),
            pltpu.make_async_copy(b_ref.at[halves[1]], basis.at[z, core, 1], own_sem.at[1]),
            pltpu.make_async_copy(d_ref.at[halves[0]], d_xy.at[y, x], own_sem.at[2]),
            pltpu.make_async_copy(d_ref.at[halves[1]], d_yx.at[x, y], own_sem.at[3]),
        ]
        for copy in kept:
            copy.start()
        for copy in kept:
            copy.wait()

    ways = [z_peer(1), z_peer(NZ - 1)]

    def origin(way, step):
        return lax.rem(z + (step if way else NZ - step), NZ)

    def hop(way, step, h):
        slot = basis.at[origin(way, step - 1), core, h]
        return remote(slot, slot, ring_s.at[way, step, h], ring_r.at[way, step, h], ways[way])

    def share(way, step, h):
        slot = basis.at[origin(way, step), core, h]
        return remote(slot, slot, sib_s.at[way, step, h], sib_r.at[way, step, h], sibling)

    for h in range(2):
        for way in range(2):
            hop(way, 1, h).start()
    xy_first = [remote(d_xy.at[y, x], d_xy.at[y, x], xy_s.at[d - 1], xy_r.at[d - 1], x_peer(d)) for d in (1, 3, 2)]
    yx_first = [remote(d_yx.at[x, y], d_yx.at[x, y], yx_s.at[d - 1], yx_r.at[d - 1], y_peer(d)) for d in (1, 3, 2)]
    for one, two in zip(xy_first, yx_first):
        one.start()
        two.start()
    for h in range(2):
        share(0, 0, h).start()

    def relay(step):
        for h in range(2):
            for way in range(2):
                hop(way, step, h).wait_recv()
                hop(way, step + 1, h).start()
                share(way, step, h).start()

    relay(1)
    for copy in xy_first:
        copy.wait_recv()
    for copy in yx_first:
        copy.wait_recv()
    xy_second = [remote(d_xy.at[y], d_xy.at[y], xy_s.at[d + 2], xy_r.at[d + 2], y_peer(d)) for d in (1, 3, 2)]
    yx_second = [remote(d_yx.at[x], d_yx.at[x], yx_s.at[d + 2], yx_r.at[d + 2], x_peer(d)) for d in (1, 3, 2)]
    for one, two in zip(xy_second, yx_second):
        one.start()
        two.start()

    @pl.loop(2, 7)
    def _(step):
        relay(step)

    for h in range(2):
        for way in range(2):
            hop(way, 7, h).wait_recv()
            if way == h:
                hop(way, 8, h).start()
            share(way, 7, h).start()
    for way in range(2):
        hop(way, 8, way).wait_recv()
        share(way, 8, way).start()

    for copy in xy_first + yx_first:
        copy.wait_send()
    for copy in xy_second + yx_second:
        copy.wait()
    for h in range(2):
        share(0, 0, h).wait()

    @pl.loop(1, 8)
    def _(step):
        for h in range(2):
            for way in range(2):
                hop(way, step, h).wait_send()
                share(way, step, h).wait()

    for way in range(2):
        hop(way, 8, way).wait_send()
        share(way, 8, way).wait()

    image_ref[...] = jnp.zeros_like(image_ref)

    @pl.loop(0, NZ)
    def _(k):
        ky, kx = lax.div(k, NX), lax.rem(k, NX)
        left = jnp.concatenate([d_xy[ky, kx], d_yx[kx, ky]], axis=0)
        right = basis[k].reshape(2 * ROWS, COLS)
        image_ref[...] += jnp.dot(left, right, preferred_element_type=jnp.float32)

    for q, (i, j) in enumerate(PAIRS):
        block = lax.dot_general(
            image_ref[:, i * TILE:(i + 1) * TILE], image_ref[:, j * TILE:(j + 1) * TILE],
            (((0,), (0,)), ((), ())), precision=HIGHEST, preferred_element_type=jnp.float32,
        )
        part[q // PER_CORE, :, q % PER_CORE] = block.reshape(NZ, PIECE, TILE)

    swap = remote(part.at[1 - core], other, pair_s.at[0], pair_r.at[0], sibling)
    swap.start()
    swap.wait_recv()
    mine[...] = part[core] + other[...]

    def scatter(d):
        to = lax.rem(z + d, NZ)
        return remote(mine.at[to], arrived.at[d], rs_s.at[d], rs_r.at[d], z_peer(d))

    @pl.loop(1, NZ)
    def _(d):
        scatter(d).start()

    total[core, z] = mine[z]

    @pl.loop(1, NZ)
    def _(d):
        scatter(d).wait_recv()
        total[core, z] += arrived[d]

    def spread(d):
        return remote(total.at[core, z], total.at[core, z], ag_s.at[d], ag_r.at[d], z_peer(d))

    @pl.loop(1, NZ)
    def _(d):
        spread(d).start()

    @pl.loop(1, NZ)
    def _(d):
        spread(d).wait_recv()

    both = remote(total.at[core], total.at[core], pair_s.at[1], pair_r.at[1], sibling)
    both.start()
    swap.wait_send()

    @pl.loop(1, NZ)
    def _(d):
        scatter(d).wait_send()
        spread(d).wait_send()

    both.wait()
    for q in range(len(PAIRS)):
        gram_ref[q] = total[q // PER_CORE, :, q % PER_CORE].reshape(TILE, TILE)


def tile_inverse(s_ref, v_ref, w_ref):
    shape = (SUB, TILE)
    row = lax.broadcasted_iota(jnp.int32, shape, 0)
    eye = lax.broadcasted_iota(jnp.int32, (TILE, TILE), 0) == lax.broadcasted_iota(jnp.int32, (TILE, TILE), 1)
    v_ref[...] = eye.astype(jnp.float32)
    for base in range(0, TILE, SUB):
        strip = s_ref[base:base + SUB, :]
        acts = v_ref[base:base + SUB, :]
        pivots = jnp.ones(shape, jnp.float32)
        for first in range(0, SUB, STEP):
            cols = [jnp.broadcast_to(strip[:, base + first + q:base + first + q + 1], shape) for q in range(STEP)]
            srows = [strip[first + q:first + q + 1, :] for q in range(STEP)]
            arows = [acts[first + q:first + q + 1, :] for q in range(STEP)]
            for q in range(STEP):
                at = first + q
                pivot = cols[q][at:at + 1, :]
                pivots = jnp.where(row == at, pivot, pivots)
                mult = jnp.where(row > at, cols[q] * (1.0 / pivot), 0.0)
                for r in range(q + 1, STEP):
                    cols[r] = cols[r] - mult * cols[r][at:at + 1, :]
                    factor = mult[first + r:first + r + 1, :]
                    srows[r] = srows[r] - factor * srows[q]
                    arows[r] = arows[r] - factor * arows[q]
                strip = strip - mult * srows[q]
                acts = acts - mult * arows[q]
        size = 1.0 / jnp.sqrt(pivots)
        upper = strip * size
        done = acts * size
        w_ref[base:base + SUB, :] = done
        if base + SUB < TILE:
            over = (((0,), (0,)), ((), ()))
            s_ref[...] -= lax.dot_general(upper, upper, over, precision=HIGHEST, preferred_element_type=jnp.float32)
            v_ref[...] -= lax.dot_general(upper, done, over, precision=HIGHEST, preferred_element_type=jnp.float32)


def mul(a, b, over):
    return lax.dot_general(a, b, (over, ((), ())), precision=HIGHEST, preferred_element_type=jnp.float32)


def refresh_kernel(gram_ref, image_ref, out_ref, a, l, w, s, v, wk):
    for q, (i, j) in enumerate(PAIRS):
        a[i, j] = gram_ref[q] * (1.0 / M)

    @pl.loop(0, NT)
    def _(k):
        s[...] = a[k, k]
        tile_inverse(s, v, wk)
        w[k, k] = wk[...]

        @pl.loop(k + 1, NT)
        def _(i):
            l[i, k] = mul(a[i, k], wk[...], ((1,), (1,)))

        @pl.loop(k + 1, NT)
        def _(i):
            @pl.loop(k + 1, i + 1)
            def _(j):
                a[i, j] = a[i, j] - mul(l[i, k], l[j, k], ((1,), (1,)))

    for i in range(1, NT):
        for j in range(i):
            acc = mul(l[i, j], w[j, j], ((1,), (0,)))
            for k in range(j + 1, i):
                acc = acc + mul(l[i, k], w[k, j], ((1,), (0,)))
            w[i, j] = -mul(w[i, i], acc, ((1,), (0,)))

    for i in range(NT):
        left = image_ref[:, 0:(i + 1) * TILE]
        right = jnp.concatenate([w[i, j] for j in range(i + 1)], axis=1)
        out_ref[:, i * TILE:(i + 1) * TILE] = mul(left, right, ((1,), (1,)))


def per_device(factor, scales, basis_block):
    f32, bf16, sem = jnp.float32, jnp.bfloat16, pltpu.SemaphoreType.DMA
    vmem = pl.BlockSpec(memory_space=pltpu.VMEM)
    image, gram = pl.pallas_call(
        gather_kernel,
        out_shape=(
            jax.ShapeDtypeStruct((ROWS, COLS), f32),
            jax.ShapeDtypeStruct((len(PAIRS), TILE, TILE), f32),
        ),
        in_specs=[vmem, vmem],
        out_specs=(vmem, vmem),
        scratch_shapes=[
            pltpu.VMEM((NY, NX, HALF, COLS), bf16),
            pltpu.VMEM((NX, NY, HALF, COLS), bf16),
            pltpu.VMEM((NZ, 2, 2, HALF, COLS), bf16),
            pltpu.VMEM((2, NZ, PER_CORE, PIECE, TILE), f32),
            pltpu.VMEM((NZ, PER_CORE, PIECE, TILE), f32),
            pltpu.VMEM((NZ, PER_CORE, PIECE, TILE), f32),
            pltpu.VMEM((NZ, PER_CORE, PIECE, TILE), f32),
            pltpu.VMEM((2, NZ, PER_CORE, PIECE, TILE), f32),
            sem((4,)), sem((4,)), sem((4,)),
            sem((6,)), sem((6,)), sem((6,)), sem((6,)),
            sem((2, 9, 2)), sem((2, 9, 2)), sem((2, 9, 2)), sem((2, 9, 2)),
            sem((2,)), sem((2,)),
            sem((NZ,)), sem((NZ,)), sem((NZ,)), sem((NZ,)),
        ],
        compiler_params=pltpu.CompilerParams(
            collective_id=0, has_side_effects=True, vmem_limit_bytes=48 * 2**20
        ),
        name="gather_gram",
    )(dequantize(factor, scales), basis_block)
    tile = pltpu.VMEM((TILE, TILE), f32)
    tiles = pltpu.VMEM((NT, NT, TILE, TILE), f32)
    result = pl.pallas_call(
        refresh_kernel,
        out_shape=jax.ShapeDtypeStruct((ROWS, COLS), f32),
        in_specs=[vmem, vmem],
        out_specs=vmem,
        scratch_shapes=[tiles, tiles, tiles, tile, tile, tile],
        compiler_params=pltpu.CompilerParams(vmem_limit_bytes=32 * 2**20),
        name="refresh",
    )(gram, image)
    pairs = []
    for rest in range(8):
        for z in range(NZ):
            one, two = (rest * 2 + 1) * 32 + z * 2, (rest * 2) * 32 + z * 2 + 1
            pairs += [(one, two), (two, one)]
    back = lax.ppermute(result, ("blk", "grp"), pairs)
    _, _, x_lo, _, core = place()
    return jnp.where(x_lo == core, result, back)


def solution(mesh):
    return jax.shard_map(
        per_device,
        mesh=mesh,
        in_specs=(P("grp", "blk"), P("grp", "blk"), P("grp", "blk")),
        out_specs=P("grp", "blk"),
        check_vma=False,
    )
```

time: 709 us -> 161 us (0.23)
  the two profiles are of different devices: /device:TPU:16 before, /device:TPU:46 now
where the time goes in v1:
time: 161 us
  Pallas kernels  147 us (91%)
  waiting for transfers between devices  8.56 us (5%)
  starting transfers between devices  1.92 us (1%)
  local copies, waits for them, and re-layouts  1.83 us (1%)
    pallas_call x1, Pallas kernels, per_device(): pl.pallas_call(gather_kernel, out_shape=(jax.ShapeDtypeStruct((ROWS, COLS...  116 us
    pallas_call x1, Pallas kernels, per_device(): pl.pallas_call(refresh_kernel, out_shape=jax.ShapeDtypeStruct((ROWS, COLS...  31.1 us
    ppermute x1, waiting for transfers between devices, per_device(): back = lax.ppermute(result, ('blk', 'grp'), pairs)  8.56 us
  transfers between devices with their start and end apart: 1, of which 1 were waited for; matrix products, arithmetic and copies ran while one was open for 0% of the time, Pallas kernels for 0%

profile of v1, /device:TPU:46, one launch (start us, length us, event | category | flops | bytes accessed | tf_op | source)
XLA Modules:
  0.0 160.5 jit_solution(8548013065619684239)
XLA Ops:
  0.0 0.0 copy-start.1
  0.0 0.9 mul.11
  0.9 0.1 copy-done.1
  1.0 0.0 copy-start
  1.0 0.1 fusion.d_ref
  1.1 0.9 copy-done
  1.9 116.1 %gather_gram.1 = (f32[256,512]{1,0:T(8,128)S(1)}, f32[10,128,128]{2,1,0:T(8,128)S(1)}) custom-call(bf16[256,512]{1,0:T(8,128)(2,1)S(1)} %fusion.d_ref, bf16[256,512]{1,0:T(8,128)(2,1)S(1)} %copy-done), custom_call_target="tpu_custom_call" | custom-call | tf_op jit(solution)/shard_map/gather_gram/pallas_call | solution.py:332
  118.0 31.1 %refresh.1 = f32[256,512]{1,0:T(8,128)S(1)} custom-call(f32[10,128,128]{2,1,0:T(8,128)S(1)} %get-tuple-element.7.gram_ref, f32[256,512]{1,0:T(8,128)S(1)} %get-tuple-element.8.image_ref), custom_call_target="tpu_custom_call" | custom-call | tf_op jit(solution)/shard_map/refresh/pallas_call | solution.py:362
  149.2 1.9 %collective-permute-start = (f32[256,512]{1,0:T(8,128)S(1)}, f32[256,512]{1,0:T(8,128)S(1)}, u32[]{:S(2)}, u32[]{:S(2)}) collective-permute-start(f32[256,512]{1,0:T(8,128)S(1)} %refresh.1), channel_id=1, source_target_pairs={{32,1},{1,32},{34,3},{3,34},{36,5},{5,36},{38,7},{7,38},{40,9},{9,... | collective-permute-start | bytes 1572872 | tf_op jit(solution)/shard_map/ppermute | solution.py:376
  151.1 8.6 %collective-permute-done = f32[256,512]{1,0:T(8,128)S(1)} collective-permute-done((f32[256,512]{1,0:T(8,128)S(1)}, f32[256,512]{1,0:T(8,128)S(1)}, u32[]{:S(2)}, u32[]{:S(2)}) %collective-permute-start) | collective-permute-done | bytes 524320 | tf_op jit(solution)/shard_map/ppermute | solution.py:376
  159.7 0.9 broadcast_select_fusion
Async XLA Ops:
  0.0 1.0 copy-start.1
  1.0 0.9 copy-start
  149.2 10.5 %collective-permute-start = (f32[256,512]{1,0:T(8,128)S(1)}, f32[256,512]{1,0:T(8,128)S(1)}, u32[]{:S(2)}, u32[]{:S(2)}) collective-permute-start(f32[256,512]{1,0:T(8,128)S(1)} %refresh.1), channel_id=1, source_target_pairs={{32,1},{1,32},{34,3},{3,34},{36,5},{5,36},{38,7},{7,38},{40,9},{9,... | collective-permute-start | bytes 1572872 | tf_op jit(solution)/shard_map/ppermute | solution.py:376

commit v2 on v1

v2 whole, which is shorter than its diff:
```python
import jax
import jax.numpy as jnp
from jax import lax
from jax.experimental import pallas as pl
from jax.experimental.pallas import tpu as pltpu
from jax.sharding import PartitionSpec as P

M = 8192
NY, NX, NZ = 4, 4, 16
ROWS, COLS = 256, 512
HALF = ROWS // 2
TILE = 128
NT = COLS // TILE
PAIRS = [(i, j) for i in range(NT) for j in range(i + 1)]
PER_CORE = len(PAIRS) // 2
PIECE = TILE // NZ
SUB = 32
STEP = 4
HIGHEST = lax.Precision.HIGHEST


def dequantize(quantized, scale_block):
    row_groups, col_groups = scale_block.shape
    width = quantized.shape[0] // row_groups
    shaped = quantized.astype(jnp.float32).reshape(row_groups, width, col_groups, width)
    return (shaped * scale_block[:, None, :, None]).reshape(quantized.shape).astype(jnp.bfloat16)


def place():
    blk, grp = lax.axis_index("blk"), lax.axis_index("grp")
    core, x_hi, y = lax.rem(blk, 2), lax.rem(lax.div(blk, 2), 2), lax.div(blk, 4)
    z, x_lo = lax.div(grp, 2), lax.rem(grp, 2)
    return y, x_hi, x_lo, z, core


def device(y, x, z, core):
    return {"blk": (y * 2 + lax.div(x, 2)) * 2 + core, "grp": z * 2 + lax.rem(x, 2)}


def remote(src, dst, send, recv, to):
    return pltpu.make_async_remote_copy(
        src_ref=src, dst_ref=dst, send_sem=send, recv_sem=recv,
        device_id=to, device_id_type=pl.DeviceIdType.MESH,
    )


def gather_kernel(
    d_ref, b_ref, image_ref, gram_ref,
    d_xy, d_yx, basis, image, image_in, part, other, mine, near, far, summed, total,
    own_sem, swap_s, swap_r, xy_s, xy_r, yx_s, yx_r, ring_s, ring_r, sib_s, sib_r,
    pair_s, pair_r, rs_s, rs_r, ag_s, ag_r, across_s, across_r,
):
    y, x_hi, x_lo, z, core = place()
    x = x_hi * 2 + x_lo
    sibling = device(y, x, z, 1 - core)
    partner_x = x_hi * 2 + core
    partner = device(y, partner_x, z, x_lo)
    moved = x_lo != core
    twin = device(y, x_hi * 2 + 1 - x_lo, z, core)

    def x_peer(d):
        return device(y, lax.rem(x + d, NX), z, core)

    def y_peer(d):
        return device(lax.rem(y + d, NY), x, z, core)

    def z_peer(d):
        return device(y, x, lax.rem(z + d, NZ), core)

    barrier = pltpu.get_barrier_semaphore()

    def greet(to):
        pl.semaphore_signal(barrier, inc=1, device_id=to, device_id_type=pl.DeviceIdType.MESH)

    greet(sibling)
    for d in range(1, 4):
        greet(x_peer(d))
        greet(y_peer(d))
    for d in (1, 15, 2, 14, 4, 8, 12):
        greet(z_peer(d))

    @pl.when(moved)
    def _():
        greet(partner)
        pl.semaphore_wait(barrier, 15)

    @pl.when(jnp.logical_not(moved))
    def _():
        pl.semaphore_wait(barrier, 14)

    halves = [pl.ds(0, HALF), pl.ds(HALF, HALF)]

    @pl.when(moved)
    def _():
        sent = [
            remote(b_ref.at[halves[0]], basis.at[z, x_lo, 0], swap_s.at[0], swap_r.at[0], partner),
            remote(b_ref.at[halves[1]], basis.at[z, x_lo, 1], swap_s.at[1], swap_r.at[1], partner),
            remote(d_ref.at[halves[0]], d_xy.at[y, partner_x], swap_s.at[2], swap_r.at[2], partner),
            remote(d_ref.at[halves[1]], d_yx.at[partner_x, y], swap_s.at[3], swap_r.at[3], partner),
        ]
        for copy in sent:
            copy.start()
        for copy in sent:
            copy.wait()

    @pl.when(jnp.logical_not(moved))
    def _():
        kept = [
            pltpu.make_async_copy(b_ref.at[halves[0]], basis.at[z, core, 0], own_sem.at[0]),
            pltpu.make_async_copy(b_ref.at[halves[1]], basis.at[z, core, 1], own_sem.at[1]),
            pltpu.make_async_copy(d_ref.at[halves[0]], d_xy.at[y, x], own_sem.at[2]),
            pltpu.make_async_copy(d_ref.at[halves[1]], d_yx.at[x, y], own_sem.at[3]),
        ]
        for copy in kept:
            copy.start()
        for copy in kept:
            copy.wait()

    ways = [z_peer(1), z_peer(NZ - 1)]

    def origin(way, step):
        return lax.rem(z + (step if way else NZ - step), NZ)

    def hop(way, step, h):
        slot = basis.at[origin(way, step - 1), core, h]
        return remote(slot, slot, ring_s.at[way, step, h], ring_r.at[way, step, h], ways[way])

    def share(way, step, h):
        slot = basis.at[origin(way, step), core, h]
        return remote(slot, slot, sib_s.at[way, step, h], sib_r.at[way, step, h], sibling)

    for h in range(2):
        for way in range(2):
            hop(way, 1, h).start()
    xy_first = [remote(d_xy.at[y, x], d_xy.at[y, x], xy_s.at[d - 1], xy_r.at[d - 1], x_peer(d)) for d in (1, 3, 2)]
    yx_first = [remote(d_yx.at[x, y], d_yx.at[x, y], yx_s.at[d - 1], yx_r.at[d - 1], y_peer(d)) for d in (1, 3, 2)]
    for one, two in zip(xy_first, yx_first):
        one.start()
        two.start()
    for h in range(2):
        share(0, 0, h).start()

    def relay(step):
        for h in range(2):
            for way in range(2):
                hop(way, step, h).wait_recv()
                hop(way, step + 1, h).start()
                share(way, step, h).start()

    relay(1)
    for copy in xy_first:
        copy.wait_recv()
    for copy in yx_first:
        copy.wait_recv()
    xy_second = [remote(d_xy.at[y], d_xy.at[y], xy_s.at[d + 2], xy_r.at[d + 2], y_peer(d)) for d in (1, 3, 2)]
    yx_second = [remote(d_yx.at[x], d_yx.at[x], yx_s.at[d + 2], yx_r.at[d + 2], x_peer(d)) for d in (1, 3, 2)]
    for one, two in zip(xy_second, yx_second):
        one.start()
        two.start()

    image[...] = jnp.zeros_like(image)

    @pl.loop(2, 6)
    def _(step):
        relay(step)

    for copy in xy_second + yx_second:
        copy.wait_recv()

    def product(k):
        ky, kx = lax.div(k, NX), lax.rem(k, NX)
        left = jnp.concatenate([d_xy[ky, kx], d_yx[kx, ky]], axis=0)
        right = basis[k].reshape(2 * ROWS, COLS)
        return jnp.dot(left, right, preferred_element_type=jnp.float32)

    def multiply(first, end):
        @pl.loop(first, end)
        def _(step):
            for h in range(2):
                for way in range(2):
                    share(way, step, h).wait_recv()
            image[...] += product(origin(0, step)) + product(origin(1, step))

    for h in range(2):
        share(0, 0, h).wait_recv()
    image[...] += product(z)
    multiply(1, 2)
    relay(6)
    multiply(2, 5)
    for h in range(2):
        for way in range(2):
            hop(way, 7, h).wait_recv()
            if way == h:
                hop(way, 8, h).start()
            share(way, 7, h).start()
    multiply(5, 7)
    for way in range(2):
        hop(way, 8, way).wait_recv()
        share(way, 8, way).start()
    multiply(7, 8)
    for way in range(2):
        share(way, 8, way).wait_recv()
    image[...] += product(origin(0, 8))

    send_image = remote(image, image_in, swap_s.at[4], swap_r.at[4], partner)

    @pl.when(moved)
    def _():
        send_image.start()

    for top in (0, 2):
        width = (top + 2) * TILE
        block = lax.dot_general(
            image[:, top * TILE:width], image[:, 0:width],
            (((0,), (0,)), ((), ())), precision=HIGHEST, preferred_element_type=jnp.float32,
        )
        for q, (i, j) in enumerate(PAIRS):
            if top <= i < top + 2:
                for t in range(NZ):
                    at = (i - top) * TILE + t * PIECE
                    part[q // PER_CORE, t % 4, t // 4, q % PER_CORE] = block[at:at + PIECE, j * TILE:(j + 1) * TILE]

    swap = remote(part.at[1 - core], other, pair_s.at[0], pair_r.at[0], sibling)
    swap.start()
    z_q, z_r = lax.div(z, 4), lax.rem(z, 4)
    offsets = (0, 1, NZ - 1, lax.rem(2 + 12 * core, NZ))
    swap.wait_recv()
    mine[...] = part[core] + other[...]
    to_near = [
        remote(mine.at[lax.rem(z_r + offsets[n], 4)], near.at[n], rs_s.at[n], rs_r.at[n], z_peer(offsets[n]))
        for n in (1, 2, 3)
    ]
    for copy in to_near:
        copy.start()
    for copy in to_near:
        copy.wait_recv()
    near[0] = mine[z_r] + near[1] + near[2] + near[3]
    to_far = [
        remote(near.at[0, lax.rem(z_q + d, 4)], far.at[d], rs_s.at[3 + d], rs_r.at[3 + d], z_peer(4 * d))
        for d in (1, 2, 3)
    ]
    for copy in to_far:
        copy.start()
    for copy in to_far:
        copy.wait_recv()
    summed[...] = near[0, z_q] + far[1] + far[2] + far[3]

    hand = remote(summed, total.at[core, z_r, z_q], swap_s.at[5], swap_r.at[5], partner)

    @pl.when(moved)
    def _():
        hand.start()
        hand.wait_recv()

    @pl.when(jnp.logical_not(moved))
    def _():
        total[core, z_r, z_q] = summed[...]

    own = total.at[x_lo, z_r, z_q]
    spread_far = [remote(own, own, ag_s.at[d], ag_r.at[d], z_peer(4 * d)) for d in (1, 2, 3)]
    for copy in spread_far:
        copy.start()
    for copy in spread_far:
        copy.wait_recv()
    group = total.at[x_lo, z_r]
    spread_near = [
        remote(group, group, ag_s.at[3 + n], ag_r.at[3 + n], z_peer(offsets[n])) for n in (1, 2, 3)
    ]
    for copy in spread_near:
        copy.start()

    def cross(n):
        slot = total.at[x_lo, lax.rem(z_r + NZ - offsets[n], 4)]
        return remote(slot, slot, across_s.at[n], across_r.at[n], twin)

    crossing = [cross(n) for n in range(4)]
    crossing[0].start()
    for n in (1, 2, 3):
        spread_near[n - 1].wait_recv()
        crossing[n].start()

    for copy in xy_first + yx_first + xy_second + yx_second:
        copy.wait_send()
    for h in range(2):
        share(0, 0, h).wait_send()

    @pl.loop(1, 8)
    def _(step):
        for h in range(2):
            for way in range(2):
                hop(way, step, h).wait_send()
                share(way, step, h).wait_send()

    for way in range(2):
        hop(way, 8, way).wait_send()
        share(way, 8, way).wait_send()
    swap.wait_send()
    for copy in to_near + to_far + spread_far + spread_near:
        copy.wait_send()

    @pl.when(moved)
    def _():
        hand.wait_send()
        send_image.wait()
        image_ref[...] = image_in[...]

    @pl.when(jnp.logical_not(moved))
    def _():
        image_ref[...] = image[...]

    for copy in crossing:
        copy.wait()
    for q in range(len(PAIRS)):
        for t in range(NZ):
            gram_ref[q, t * PIECE:(t + 1) * PIECE, :] = total[q // PER_CORE, t % 4, t // 4, q % PER_CORE]


def tile_inverse(s_ref, v_ref, w_ref):
    vreg = (8, TILE)
    groups = SUB // 8
    row = lax.broadcasted_iota(jnp.int32, vreg, 0)
    eye = lax.broadcasted_iota(jnp.int32, (TILE, TILE), 0) == lax.broadcasted_iota(jnp.int32, (TILE, TILE), 1)
    v_ref[...] = eye.astype(jnp.float32)
    spread = lambda value: jnp.broadcast_to(value, vreg)
    for base in range(0, TILE, SUB):
        strip = [s_ref[base + 8 * g:base + 8 * g + 8, :] for g in range(groups)]
        acts = [v_ref[base + 8 * g:base + 8 * g + 8, :] for g in range(groups)]
        pivots = [jnp.ones(vreg, jnp.float32) for _ in range(groups)]
        for first in range(0, SUB, STEP):
            g0, r0, c0 = first // 8, first % 8, base + first
            live = range(g0, groups)
            srows = [spread(strip[g0][r0 + q:r0 + q + 1, :]) for q in range(STEP)]
            arows = [spread(acts[g0][r0 + q:r0 + q + 1, :]) for q in range(STEP)]
            cols = [{g: spread(strip[g][:, c0 + q:c0 + q + 1]) for g in live} for q in range(STEP)]
            block = {
                (q, r): spread(srows[q][:, c0 + r:c0 + r + 1]) for q in range(STEP) for r in range(q, STEP)
            }
            for q in range(STEP):
                inv = 1.0 / block[q, q]
                pivots[g0] = jnp.where(row == r0 + q, block[q, q], pivots[g0])
                factor = {r: block[q, r] * inv for r in range(q + 1, STEP)}
                for r in range(q + 1, STEP):
                    for t in range(r, STEP):
                        block[r, t] = block[r, t] - factor[r] * block[q, t]
                for g in live:
                    mult = cols[q][g] * inv
                    for r in range(q + 1, STEP):
                        cols[r][g] = cols[r][g] - mult * block[q, r]
                    if g == g0:
                        mult = jnp.where(row > r0 + q, mult, 0.0)
                    strip[g] = strip[g] - mult * srows[q]
                    acts[g] = acts[g] - mult * arows[q]
                for r in range(q + 1, STEP):
                    srows[r] = srows[r] - factor[r] * srows[q]
                    arows[r] = arows[r] - factor[r] * arows[q]
        size = [1.0 / jnp.sqrt(p) for p in pivots]
        upper = jnp.concatenate([s * n for s, n in zip(strip, size)], axis=0)
        done = jnp.concatenate([s * n for s, n in zip(acts, size)], axis=0)
        w_ref[base:base + SUB, :] = done
        below = base + SUB
        if below < TILE:
            s_ref[below:, :] -= mul(upper[:, below:], upper, ((0,), (0,)))
            v_ref[below:, :] -= mul(upper[:, below:], done, ((0,), (0,)))


def mul(a, b, over):
    return lax.dot_general(a, b, (over, ((), ())), precision=HIGHEST, preferred_element_type=jnp.float32)


def refresh_kernel(gram_ref, image_ref, out_ref, a, w, v, s, vt):
    for q, (i, j) in enumerate(PAIRS):
        a[i * TILE:(i + 1) * TILE, j * TILE:(j + 1) * TILE] = gram_ref[q] * (1.0 / M)

    for k in range(NT):
        k0, k1 = k * TILE, (k + 1) * TILE
        s[...] = a[k0:k1, k0:k1]
        tile_inverse(s, vt, w.at[k0:k1, k0:k1])
        wk = w[k0:k1, k0:k1]
        if k < NT - 1:
            panel = mul(a[k1:, k0:k1], wk, ((1,), (1,)))
            for j in range(k + 1, NT):
                j0, j1 = j * TILE, (j + 1) * TILE
                a[j0:, j0:j1] -= mul(panel[j0 - k1:], panel[j0 - k1:j1 - k1], ((1,), (1,)))
        if k > 0:
            w[k0:k1, 0:k0] = mul(wk, v[k0:k1, 0:k0], ((1,), (0,)))
        if k < NT - 1:
            v[k1:, k0:k1] = -mul(panel, wk, ((1,), (0,)))
            if k > 0:
                v[k1:, 0:k0] -= mul(panel, w[k0:k1, 0:k0], ((1,), (0,)))
        out_ref[:, k0:k1] = mul(image_ref[:, 0:k1], w[k0:k1, 0:k1], ((1,), (1,)))


def per_device(factor, scales, basis_block):
    f32, bf16, sem = jnp.float32, jnp.bfloat16, pltpu.SemaphoreType.DMA
    vmem = pl.BlockSpec(memory_space=pltpu.VMEM)
    image, gram = pl.pallas_call(
        gather_kernel,
        out_shape=(
            jax.ShapeDtypeStruct((ROWS, COLS), f32),
            jax.ShapeDtypeStruct((len(PAIRS), TILE, TILE), f32),
        ),
        in_specs=[vmem, vmem],
        out_specs=(vmem, vmem),
        scratch_shapes=[
            pltpu.VMEM((NY, NX, HALF, COLS), bf16),
            pltpu.VMEM((NX, NY, HALF, COLS), bf16),
            pltpu.VMEM((NZ, 2, 2, HALF, COLS), bf16),
            pltpu.VMEM((ROWS, COLS), f32),
            pltpu.VMEM((ROWS, COLS), f32),
            pltpu.VMEM((2, 4, 4, PER_CORE, PIECE, TILE), f32),
            pltpu.VMEM((4, 4, PER_CORE, PIECE, TILE), f32),
            pltpu.VMEM((4, 4, PER_CORE, PIECE, TILE), f32),
            pltpu.VMEM((4, 4, PER_CORE, PIECE, TILE), f32),
            pltpu.VMEM((4, PER_CORE, PIECE, TILE), f32),
            pltpu.VMEM((PER_CORE, PIECE, TILE), f32),
            pltpu.VMEM((2, 4, 4, PER_CORE, PIECE, TILE), f32),
            sem((4,)), sem((6,)), sem((6,)),
            sem((6,)), sem((6,)), sem((6,)), sem((6,)),
            sem((2, 9, 2)), sem((2, 9, 2)), sem((2, 9, 2)), sem((2, 9, 2)),
            sem((1,)), sem((1,)),
            sem((7,)), sem((7,)), sem((7,)), sem((7,)),
            sem((4,)), sem((4,)),
        ],
        compiler_params=pltpu.CompilerParams(
            collective_id=0, has_side_effects=True, vmem_limit_bytes=48 * 2**20
        ),
        name="gather_gram",
    )(dequantize(factor, scales), basis_block)
    tile = pltpu.VMEM((TILE, TILE), f32)
    square = pltpu.VMEM((COLS, COLS), f32)
    return pl.pallas_call(
        refresh_kernel,
        out_shape=jax.ShapeDtypeStruct((ROWS, COLS), f32),
        in_specs=[vmem, vmem],
        out_specs=vmem,
        scratch_shapes=[square, square, square, tile, tile],
        compiler_params=pltpu.CompilerParams(vmem_limit_bytes=32 * 2**20),
        name="refresh",
    )(gram, image)


def solution(mesh):
    return jax.shard_map(
        per_device,
        mesh=mesh,
        in_specs=(P("grp", "blk"), P("grp", "blk"), P("grp", "blk")),
        out_specs=P("grp", "blk"),
        check_vma=False,
    )
```

time: 161 us -> 139 us (0.86)
  the two profiles are of different devices: /device:TPU:46 before, /device:TPU:8 now
where the time goes in v2:
time: 139 us
  Pallas kernels  137 us (99%)
  local copies, waits for them, and re-layouts  1.83 us (1%)
    pallas_call x1, Pallas kernels, per_device(): pl.pallas_call(gather_kernel, out_shape=(jax.ShapeDtypeStruct((ROWS, COLS...  109 us
    pallas_call x1, Pallas kernels, per_device(): pl.pallas_call(refresh_kernel, out_shape=jax.ShapeDtypeStruct((ROWS, COLS...  28 us

profile of v2, /device:TPU:8, one launch (start us, length us, event | category | flops | bytes accessed | tf_op | source)
XLA Modules:
  0.0 138.8 jit_solution(9130671975892010482)
XLA Ops:
  0.0 0.0 copy-start.1
  0.0 0.9 mul.11
  0.9 0.1 copy-done.1
  1.0 0.0 copy-start
  1.0 0.1 fusion.d_ref
  1.1 0.9 copy-done
  1.9 108.9 %gather_gram.1 = (f32[256,512]{1,0:T(8,128)S(1)}, f32[10,128,128]{2,1,0:T(8,128)S(1)}) custom-call(bf16[256,512]{1,0:T(8,128)(2,1)S(1)} %fusion.d_ref, bf16[256,512]{1,0:T(8,128)(2,1)S(1)} %copy-done), custom_call_target="tpu_custom_call" | custom-call | tf_op jit(solution)/shard_map/gather_gram/pallas_call | solution.py:396
  110.8 28.0 %refresh.1 = f32[256,512]{1,0:T(8,128)} custom-call(f32[10,128,128]{2,1,0:T(8,128)S(1)} %get-tuple-element.7.gram_ref, f32[256,512]{1,0:T(8,128)S(1)} %get-tuple-element.8.image_ref), custom_call_target="tpu_custom_call" | custom-call | tf_op jit(solution)/shard_map/refresh/pallas_call | solution.py:431
Async XLA Ops:
  0.0 1.0 copy-start.1
  1.0 0.9 copy-start

commit v3 on v2

--- a/solution.py
+++ b/solution.py
@@ -14,16 +14,9 @@
 PAIRS = [(i, j) for i in range(NT) for j in range(i + 1)]
 PER_CORE = len(PAIRS) // 2
 PIECE = TILE // NZ
-SUB = 32
+SUB = 64
 STEP = 4
 HIGHEST = lax.Precision.HIGHEST
-
-
-def dequantize(quantized, scale_block):
-    row_groups, col_groups = scale_block.shape
-    width = quantized.shape[0] // row_groups
-    shaped = quantized.astype(jnp.float32).reshape(row_groups, width, col_groups, width)
-    return (shaped * scale_block[:, None, :, None]).reshape(quantized.shape).astype(jnp.bfloat16)
 
 
 def place():
@@ -45,8 +38,8 @@
 
 
 def gather_kernel(
-    d_ref, b_ref, image_ref, gram_ref,
-    d_xy, d_yx, basis, image, image_in, part, other, mine, near, far, summed, total,
+    f_ref, scale_ref, b_ref, image_ref, gram_ref,
+    f_in, dequant, d_xy, d_yx, basis, image, image_in, part, other, mine, near, far, summed, total,
     own_sem, swap_s, swap_r, xy_s, xy_r, yx_s, yx_r, ring_s, ring_r, sib_s, sib_r,
     pair_s, pair_r, rs_s, rs_r, ag_s, ag_r, across_s, across_r,
 ):
@@ -67,6 +60,8 @@
     def z_peer(d):
         return device(y, x, lax.rem(z + d, NZ), core)
 
+    load = pltpu.make_async_copy(f_ref, f_in, own_sem.at[4])
+    load.start()
     barrier = pltpu.get_barrier_semaphore()
 
     def greet(to):
@@ -82,6 +77,15 @@
     @pl.when(moved)
     def _():
         greet(partner)
+
+    load.wait()
+    for i in range(ROWS // TILE):
+        for j in range(NT):
+            at = (slice(i * TILE, (i + 1) * TILE), slice(j * TILE, (j + 1) * TILE))
+            dequant[at] = (f_in[at].astype(jnp.float32) * scale_ref[i, j]).astype(jnp.bfloat16)
+
+    @pl.when(moved)
+    def _():
         pl.semaphore_wait(barrier, 15)
 
     @pl.when(jnp.logical_not(moved))
@@ -89,31 +93,33 @@
         pl.semaphore_wait(barrier, 14)
 
     halves = [pl.ds(0, HALF), pl.ds(HALF, HALF)]
-
-    @pl.when(moved)
-    def _():
-        sent = [
-            remote(b_ref.at[halves[0]], basis.at[z, x_lo, 0], swap_s.at[0], swap_r.at[0], partner),
-            remote(b_ref.at[halves[1]], basis.at[z, x_lo, 1], swap_s.at[1], swap_r.at[1], partner),
-            remote(d_ref.at[halves[0]], d_xy.at[y, partner_x], swap_s.at[2], swap_r.at[2], partner),
-            remote(d_ref.at[halves[1]], d_yx.at[partner_x, y], swap_s.at[3], swap_r.at[3], partner),
-        ]
-        for copy in sent:
+    swap_b = [
+        remote(b_ref.at[halves[h]], basis.at[z, x_lo, h], swap_s.at[h], swap_r.at[h], partner) for h in range(2)
+    ]
+    swap_d = [
+        remote(dequant.at[halves[0]], d_xy.at[y, partner_x], swap_s.at[2], swap_r.at[2], partner),
+        remote(dequant.at[halves[1]], d_yx.at[partner_x, y], swap_s.at[3], swap_r.at[3], partner),
+    ]
+    kept_b = [pltpu.make_async_copy(b_ref.at[halves[h]], basis.at[z, core, h], own_sem.at[h]) for h in range(2)]
+    kept_d = [
+        pltpu.make_async_copy(dequant.at[halves[0]], d_xy.at[y, x], own_sem.at[2]),
+        pltpu.make_async_copy(dequant.at[halves[1]], d_yx.at[x, y], own_sem.at[3]),
+    ]
+
+    @pl.when(moved)
+    def _():
+        for copy in swap_b:
             copy.start()
-        for copy in sent:
+        for copy in swap_b:
             copy.wait()
+        for copy in swap_d:
+            copy.start()
 
     @pl.when(jnp.logical_not(moved))
     def _():
-        kept = [
-            pltpu.make_async_copy(b_ref.at[halves[0]], basis.at[z, core, 0], own_sem.at[0]),
-            pltpu.make_async_copy(b_ref.at[halves[1]], basis.at[z, core, 1], own_sem.at[1]),
-            pltpu.make_async_copy(d_ref.at[halves[0]], d_xy.at[y, x], own_sem.at[2]),
-            pltpu.make_async_copy(d_ref.at[halves[1]], d_yx.at[x, y], own_sem.at[3]),
-        ]
-        for copy in kept:
+        for copy in kept_b + kept_d:
             copy.start()
-        for copy in kept:
+        for copy in kept_b:
             copy.wait()
 
     ways = [z_peer(1), z_peer(NZ - 1)]
@@ -132,13 +138,53 @@
     for h in range(2):
         for way in range(2):
             hop(way, 1, h).start()
-    xy_first = [remote(d_xy.at[y, x], d_xy.at[y, x], xy_s.at[d - 1], xy_r.at[d - 1], x_peer(d)) for d in (1, 3, 2)]
-    yx_first = [remote(d_yx.at[x, y], d_yx.at[x, y], yx_s.at[d - 1], yx_r.at[d - 1], y_peer(d)) for d in (1, 3, 2)]
-    for one, two in zip(xy_first, yx_first):
-        one.start()
-        two.start()
     for h in range(2):
         share(0, 0, h).start()
+
+    @pl.when(moved)
+    def _():
+        for copy in swap_d:
+            copy.wait()
+
+    @pl.when(jnp.logical_not(moved))
+    def _():
+        for copy in kept_d:
+            copy.wait()
+
+    def both_ways(refs, send, recv, to):
+        return [remote(refs[n], refs[n], send.at[n], recv.at[n], to[n]) for n in (0, 1)]
+
+    x_next, y_next = [x_peer(1), x_peer(NX - 1)], [y_peer(1), y_peer(NY - 1)]
+    x_back, x_on = lax.rem(x + NX - 1, NX), lax.rem(x + 1, NX)
+    y_back, y_on = lax.rem(y + NY - 1, NY), lax.rem(y + 1, NY)
+    quarter = [pl.ds(0, HALF // 2), pl.ds(HALF // 2, HALF // 2)]
+    pair = [pl.ds(0, 2), pl.ds(2, 2)]
+    first = (
+        both_ways([d_xy.at[y, x]] * 2, xy_s.at[0], xy_r.at[0], x_next)
+        + both_ways([d_yx.at[x, y]] * 2, yx_s.at[0], yx_r.at[0], y_next)
+    )
+    first_on = (
+        both_ways([d_xy.at[y, x_back, quarter[0]], d_xy.at[y, x_on, quarter[1]]], xy_s.at[1], xy_r.at[1], x_next)
+        + both_ways([d_yx.at[x, y_back, quarter[0]], d_yx.at[x, y_on, quarter[1]]], yx_s.at[1], yx_r.at[1], y_next)
+    )
+    second = (
+        both_ways([d_xy.at[y]] * 2, xy_s.at[2], xy_r.at[2], y_next)
+        + both_ways([d_yx.at[x]] * 2, yx_s.at[2], yx_r.at[2], x_next)
+    )
+    second_on = (
+        both_ways([d_xy.at[y_back, pair[0]], d_xy.at[y_on, pair[1]]], xy_s.at[3], xy_r.at[3], y_next)
+        + both_ways([d_yx.at[x_back, pair[0]], d_yx.at[x_on, pair[1]]], yx_s.at[3], yx_r.at[3], x_next)
+    )
+
+    def start(copies):
+        for copy in copies:
+            copy.start()
+
+    def land(copies):
+        for copy in copies:
+            copy.wait_recv()
+
+    start(first)
 
     def relay(step):
         for h in range(2):
@@ -148,24 +194,19 @@
                 share(way, step, h).start()
 
     relay(1)
-    for copy in xy_first:
-        copy.wait_recv()
-    for copy in yx_first:
-        copy.wait_recv()
-    xy_second = [remote(d_xy.at[y], d_xy.at[y], xy_s.at[d + 2], xy_r.at[d + 2], y_peer(d)) for d in (1, 3, 2)]
-    yx_second = [remote(d_yx.at[x], d_yx.at[x], yx_s.at[d + 2], yx_r.at[d + 2], x_peer(d)) for d in (1, 3, 2)]
-    for one, two in zip(xy_second, yx_second):
-        one.start()
-        two.start()
-
+    land(first)
+    start(first_on)
+    relay(2)
+    land(first_on)
+    start(second)
     image[...] = jnp.zeros_like(image)
-
-    @pl.loop(2, 6)
-    def _(step):
-        relay(step)
-
-    for copy in xy_second + yx_second:
-        copy.wait_recv()
+    relay(3)
+    relay(4)
+    land(second)
+    start(second_on)
+    relay(5)
+    relay(6)
+    land(second_on)
 
     def product(k):
         ky, kx = lax.div(k, NX), lax.rem(k, NX)
@@ -184,20 +225,18 @@
     for h in range(2):
         share(0, 0, h).wait_recv()
     image[...] += product(z)
-    multiply(1, 2)
-    relay(6)
-    multiply(2, 5)
+    multiply(1, 3)
     for h in range(2):
         for way in range(2):
             hop(way, 7, h).wait_recv()
             if way == h:
                 hop(way, 8, h).start()
             share(way, 7, h).start()
-    multiply(5, 7)
+    multiply(3, 6)
     for way in range(2):
         hop(way, 8, way).wait_recv()
         share(way, 8, way).start()
-    multiply(7, 8)
+    multiply(6, 8)
     for way in range(2):
         share(way, 8, way).wait_recv()
     image[...] += product(origin(0, 8))
@@ -279,7 +318,7 @@
         spread_near[n - 1].wait_recv()
         crossing[n].start()
 
-    for copy in xy_first + yx_first + xy_second + yx_second:
+    for copy in first + first_on + second + second_on:
         copy.wait_send()
     for h in range(2):
         share(0, 0, h).wait_send()
@@ -399,9 +438,15 @@
             jax.ShapeDtypeStruct((ROWS, COLS), f32),
             jax.ShapeDtypeStruct((len(PAIRS), TILE, TILE), f32),
         ),
-        in_specs=[vmem, vmem],
+        in_specs=[
+            pl.BlockSpec(memory_space=pl.ANY),
+            pl.BlockSpec(memory_space=pltpu.SMEM),
+            pl.BlockSpec(memory_space=pl.ANY),
+        ],
         out_specs=(vmem, vmem),
         scratch_shapes=[
+            pltpu.VMEM((ROWS, COLS), bf16),
+            pltpu.VMEM((ROWS, COLS), bf16),
             pltpu.VMEM((NY, NX, HALF, COLS), bf16),
             pltpu.VMEM((NX, NY, HALF, COLS), bf16),
             pltpu.VMEM((NZ, 2, 2, HALF, COLS), bf16),
@@ -414,8 +459,8 @@
             pltpu.VMEM((4, PER_CORE, PIECE, TILE), f32),
             pltpu.VMEM((PER_CORE, PIECE, TILE), f32),
             pltpu.VMEM((2, 4, 4, PER_CORE, PIECE, TILE), f32),
-            sem((4,)), sem((6,)), sem((6,)),
-            sem((6,)), sem((6,)), sem((6,)), sem((6,)),
+            sem((5,)), sem((6,)), sem((6,)),
+            sem((4, 2)), sem((4, 2)), sem((4, 2)), sem((4, 2)),
             sem((2, 9, 2)), sem((2, 9, 2)), sem((2, 9, 2)), sem((2, 9, 2)),
             sem((1,)), sem((1,)),
             sem((7,)), sem((7,)), sem((7,)), sem((7,)),
@@ -425,7 +470,7 @@
             collective_id=0, has_side_effects=True, vmem_limit_bytes=48 * 2**20
         ),
         name="gather_gram",
-    )(dequantize(factor, scales), basis_block)
+    )(factor, scales, basis_block)
     tile = pltpu.VMEM((TILE, TILE), f32)
     square = pltpu.VMEM((COLS, COLS), f32)
     return pl.pallas_call(

time: 139 us -> 136 us (0.978)
  the two profiles are of different devices: /device:TPU:8 before, /device:TPU:50 now
where the time goes in v3:
time: 136 us
  Pallas kernels  134 us (99%)
  local copies, waits for them, and re-layouts  2.58 us (2%)
    pallas_call x1, Pallas kernels, per_device(): pl.pallas_call(gather_kernel, out_shape=(jax.ShapeDtypeStruct((ROWS, COLS...  107 us
    pallas_call x1, Pallas kernels, per_device(): pl.pallas_call(refresh_kernel, out_shape=jax.ShapeDtypeStruct((ROWS, COLS...  26.7 us

profile of v3, /device:TPU:50, one launch (start us, length us, event | category | flops | bytes accessed | tf_op | source)
XLA Modules:
  0.0 136.2 jit_solution(8938642113470564829)
XLA Ops:
  0.0 0.0 copy-start
  0.0 0.9 copy-done
  1.0 0.0 copy-start.1
  1.0 0.9 copy-done.1
  1.9 0.0 copy-start.2
  1.9 0.7 copy-done.2
  2.6 106.9 %gather_gram.1 = (f32[256,512]{1,0:T(8,128)S(1)}, f32[10,128,128]{2,1,0:T(8,128)S(1)}) custom-call(bf16[256,512]{1,0:T(8,128)(2,1)S(1)} %copy-done, f32[2,4]{1,0:T(2,128)S(1)} %copy-done.2, bf16[256,512]{1,0:T(8,128)(2,1)S(1)} %copy-done.1), custom_call_target="tpu_custom_call" | custom-call | tf_op jit(solution)/shard_map/gather_gram/pallas_call | solution.py:435
  109.4 26.7 %refresh.1 = f32[256,512]{1,0:T(8,128)} custom-call(f32[10,128,128]{2,1,0:T(8,128)S(1)} %get-tuple-element.7.gram_ref, f32[256,512]{1,0:T(8,128)S(1)} %get-tuple-element.8.image_ref), custom_call_target="tpu_custom_call" | custom-call | tf_op jit(solution)/shard_map/refresh/pallas_call | solution.py:476
Async XLA Ops:
  0.0 0.9 copy-start
  1.0 0.9 copy-start.1
  1.9 0.7 copy-start.2

commit v4 on v3

--- a/solution.py
+++ b/solution.py
@@ -14,8 +14,9 @@
 PAIRS = [(i, j) for i in range(NT) for j in range(i + 1)]
 PER_CORE = len(PAIRS) // 2
 PIECE = TILE // NZ
+SETS = ((0, 3), (3, 2))
 SUB = 64
-STEP = 4
+STEP = 8
 HIGHEST = lax.Precision.HIGHEST
 
 
@@ -257,66 +258,74 @@
             if top <= i < top + 2:
                 for t in range(NZ):
                     at = (i - top) * TILE + t * PIECE
-                    part[q // PER_CORE, t % 4, t // 4, q % PER_CORE] = block[at:at + PIECE, j * TILE:(j + 1) * TILE]
-
-    swap = remote(part.at[1 - core], other, pair_s.at[0], pair_r.at[0], sibling)
-    swap.start()
+                    part[q % PER_CORE // 3][q // PER_CORE, t % 4, t // 4, q % PER_CORE % 3] = (
+                        block[at:at + PIECE, j * TILE:(j + 1) * TILE]
+                    )
+
+    both = range(len(SETS))
+    swap = [remote(part[u].at[1 - core], other[u], pair_s.at[u], pair_r.at[u], sibling) for u in both]
+    start(swap)
     z_q, z_r = lax.div(z, 4), lax.rem(z, 4)
     offsets = (0, 1, NZ - 1, lax.rem(2 + 12 * core, NZ))
-    swap.wait_recv()
-    mine[...] = part[core] + other[...]
-    to_near = [
-        remote(mine.at[lax.rem(z_r + offsets[n], 4)], near.at[n], rs_s.at[n], rs_r.at[n], z_peer(offsets[n]))
+    to_near = [[
+        remote(mine[u].at[lax.rem(z_r + offsets[n], 4)], near[u].at[n], rs_s.at[u, n], rs_r.at[u, n], z_peer(offsets[n]))
         for n in (1, 2, 3)
+    ] for u in both]
+    to_far = [[
+        remote(near[u].at[0, lax.rem(z_q + d, 4)], far[u].at[d], rs_s.at[u, 3 + d], rs_r.at[u, 3 + d], z_peer(4 * d))
+        for d in (1, 2, 3)
+    ] for u in both]
+    for u in both:
+        swap[u].wait_recv()
+        mine[u][...] = part[u][core] + other[u][...]
+        start(to_near[u])
+    for u in both:
+        land(to_near[u])
+        near[u][0] = mine[u][z_r] + near[u][1] + near[u][2] + near[u][3]
+        start(to_far[u])
+
+    hand = [
+        remote(summed[u], total[u].at[core, z_r, z_q], swap_s.at[5 + u], swap_r.at[5 + u], partner) for u in both
     ]
-    for copy in to_near:
-        copy.start()
-    for copy in to_near:
-        copy.wait_recv()
-    near[0] = mine[z_r] + near[1] + near[2] + near[3]
-    to_far = [
-        remote(near.at[0, lax.rem(z_q + d, 4)], far.at[d], rs_s.at[3 + d], rs_r.at[3 + d], z_peer(4 * d))
-        for d in (1, 2, 3)
-    ]
-    for copy in to_far:
-        copy.start()
-    for copy in to_far:
-        copy.wait_recv()
-    summed[...] = near[0, z_q] + far[1] + far[2] + far[3]
-
-    hand = remote(summed, total.at[core, z_r, z_q], swap_s.at[5], swap_r.at[5], partner)
-
-    @pl.when(moved)
-    def _():
-        hand.start()
-        hand.wait_recv()
-
-    @pl.when(jnp.logical_not(moved))
-    def _():
-        total[core, z_r, z_q] = summed[...]
-
-    own = total.at[x_lo, z_r, z_q]
-    spread_far = [remote(own, own, ag_s.at[d], ag_r.at[d], z_peer(4 * d)) for d in (1, 2, 3)]
-    for copy in spread_far:
-        copy.start()
-    for copy in spread_far:
-        copy.wait_recv()
-    group = total.at[x_lo, z_r]
-    spread_near = [
-        remote(group, group, ag_s.at[3 + n], ag_r.at[3 + n], z_peer(offsets[n])) for n in (1, 2, 3)
-    ]
-    for copy in spread_near:
-        copy.start()
-
-    def cross(n):
-        slot = total.at[x_lo, lax.rem(z_r + NZ - offsets[n], 4)]
-        return remote(slot, slot, across_s.at[n], across_r.at[n], twin)
-
-    crossing = [cross(n) for n in range(4)]
-    crossing[0].start()
-    for n in (1, 2, 3):
-        spread_near[n - 1].wait_recv()
-        crossing[n].start()
+    for u in both:
+        land(to_far[u])
+        summed[u][...] = near[u][0, z_q] + far[u][1] + far[u][2] + far[u][3]
+
+        @pl.when(moved)
+        def _(u=u):
+            hand[u].start()
+
+        @pl.when(jnp.logical_not(moved))
+        def _(u=u):
+            total[u][core, z_r, z_q] = summed[u][...]
+
+    def same(ref, send, recv, to):
+        return remote(ref, ref, send, recv, to)
+
+    spread_far = [[
+        same(total[u].at[x_lo, z_r, z_q], ag_s.at[u, d], ag_r.at[u, d], z_peer(4 * d)) for d in (1, 2, 3)
+    ] for u in both]
+    spread_near = [[
+        same(total[u].at[x_lo, z_r], ag_s.at[u, 3 + n], ag_r.at[u, 3 + n], z_peer(offsets[n])) for n in (1, 2, 3)
+    ] for u in both]
+    crossing = [[
+        same(total[u].at[x_lo, lax.rem(z_r + NZ - offsets[n], 4)], across_s.at[u, n], across_r.at[u, n], twin)
+        for n in range(4)
+    ] for u in both]
+    for u in both:
+        @pl.when(moved)
+        def _(u=u):
+            hand[u].wait_recv()
+
+        start(spread_far[u])
+    for u in both:
+        land(spread_far[u])
+        start(spread_near[u])
+        crossing[u][0].start()
+    for u in both:
+        for n in (1, 2, 3):
+            spread_near[u][n - 1].wait_recv()
+            crossing[u][n].start()
 
     for copy in first + first_on + second + second_on:
         copy.wait_send()
@@ -333,13 +342,13 @@
     for way in range(2):
         hop(way, 8, way).wait_send()
         share(way, 8, way).wait_send()
-    swap.wait_send()
-    for copy in to_near + to_far + spread_far + spread_near:
+    for copy in swap + sum(to_near + to_far + spread_far + spread_near, []):
         copy.wait_send()
 
     @pl.when(moved)
     def _():
-        hand.wait_send()
+        for copy in hand:
+            copy.wait_send()
         send_image.wait()
         image_ref[...] = image_in[...]
 
@@ -347,11 +356,12 @@
     def _():
         image_ref[...] = image[...]
 
-    for copy in crossing:
+    for copy in sum(crossing, []):
         copy.wait()
     for q in range(len(PAIRS)):
         for t in range(NZ):
-            gram_ref[q, t * PIECE:(t + 1) * PIECE, :] = total[q // PER_CORE, t % 4, t // 4, q % PER_CORE]
+            piece = total[q % PER_CORE // 3][q // PER_CORE, t % 4, t // 4, q % PER_CORE % 3]
+            gram_ref[q, t * PIECE:(t + 1) * PIECE, :] = piece
 
 
 def tile_inverse(s_ref, v_ref, w_ref):
@@ -375,7 +385,12 @@
                 (q, r): spread(srows[q][:, c0 + r:c0 + r + 1]) for q in range(STEP) for r in range(q, STEP)
             }
             for q in range(STEP):
-                inv = 1.0 / block[q, q]
+                if q % 2 == 0:
+                    det = block[q, q] * block[q + 1, q + 1] - block[q, q + 1] * block[q, q + 1]
+                    inv = 1.0 / block[q, q]
+                    inv_next, pivot_next = block[q, q] * (1.0 / det), det * inv
+                else:
+                    inv, block[q, q] = inv_next, pivot_next
                 pivots[g0] = jnp.where(row == r0 + q, block[q, q], pivots[g0])
                 factor = {r: block[q, r] * inv for r in range(q + 1, STEP)}
                 for r in range(q + 1, STEP):
@@ -406,9 +421,17 @@
     return lax.dot_general(a, b, (over, ((), ())), precision=HIGHEST, preferred_element_type=jnp.float32)
 
 
-def refresh_kernel(gram_ref, image_ref, out_ref, a, w, v, s, vt):
+def refresh_kernel(gram_ref, image_ref, out_ref, a, w, v, s, vt, scaled):
+    eye = lax.broadcasted_iota(jnp.int32, (TILE, TILE), 0) == lax.broadcasted_iota(jnp.int32, (TILE, TILE), 1)
+    down, along = [], []
+    for i in range(NT):
+        diagonal = jnp.where(eye, gram_ref[PAIRS.index((i, i))] * (1.0 / M), 0.0)
+        down.append(1.0 / jnp.sqrt(jnp.sum(diagonal, axis=1, keepdims=True)))
+        along.append(1.0 / jnp.sqrt(jnp.sum(diagonal, axis=0, keepdims=True)))
     for q, (i, j) in enumerate(PAIRS):
-        a[i * TILE:(i + 1) * TILE, j * TILE:(j + 1) * TILE] = gram_ref[q] * (1.0 / M)
+        a[i * TILE:(i + 1) * TILE, j * TILE:(j + 1) * TILE] = gram_ref[q] * (1.0 / M) * down[i] * along[j]
+    for i in range(NT):
+        scaled[:, i * TILE:(i + 1) * TILE] = image_ref[:, i * TILE:(i + 1) * TILE] * along[i]
 
     for k in range(NT):
         k0, k1 = k * TILE, (k + 1) * TILE
@@ -426,7 +449,7 @@
             v[k1:, k0:k1] = -mul(panel, wk, ((1,), (0,)))
             if k > 0:
                 v[k1:, 0:k0] -= mul(panel, w[k0:k1, 0:k0], ((1,), (0,)))
-        out_ref[:, k0:k1] = mul(image_ref[:, 0:k1], w[k0:k1, 0:k1], ((1,), (1,)))
+        out_ref[:, k0:k1] = mul(scaled[:, 0:k1], w[k0:k1, 0:k1], ((1,), (1,)))
 
 
 def per_device(factor, scales, basis_block):
@@ -439,9 +462,9 @@
             jax.ShapeDtypeStruct((len(PAIRS), TILE, TILE), f32),
         ),
         in_specs=[
-            pl.BlockSpec(memory_space=pl.ANY),
+            pl.BlockSpec(memory_space=pltpu.HBM),
             pl.BlockSpec(memory_space=pltpu.SMEM),
-            pl.BlockSpec(memory_space=pl.ANY),
+            pl.BlockSpec(memory_space=pltpu.HBM),
         ],
         out_specs=(vmem, vmem),
         scratch_shapes=[
@@ -452,19 +475,16 @@
             pltpu.VMEM((NZ, 2, 2, HALF, COLS), bf16),
             pltpu.VMEM((ROWS, COLS), f32),
             pltpu.VMEM((ROWS, COLS), f32),
-            pltpu.VMEM((2, 4, 4, PER_CORE, PIECE, TILE), f32),
-            pltpu.VMEM((4, 4, PER_CORE, PIECE, TILE), f32),
-            pltpu.VMEM((4, 4, PER_CORE, PIECE, TILE), f32),
-            pltpu.VMEM((4, 4, PER_CORE, PIECE, TILE), f32),
-            pltpu.VMEM((4, PER_CORE, PIECE, TILE), f32),
-            pltpu.VMEM((PER_CORE, PIECE, TILE), f32),
-            pltpu.VMEM((2, 4, 4, PER_CORE, PIECE, TILE), f32),
-            sem((5,)), sem((6,)), sem((6,)),
+            *[
+                [pltpu.VMEM((*lead, n, PIECE, TILE), f32) for _, n in SETS]
+                for lead in ((2, 4, 4), (4, 4), (4, 4), (4, 4), (4,), (), (2, 4, 4))
+            ],
+            sem((5,)), sem((7,)), sem((7,)),
             sem((4, 2)), sem((4, 2)), sem((4, 2)), sem((4, 2)),
             sem((2, 9, 2)), sem((2, 9, 2)), sem((2, 9, 2)), sem((2, 9, 2)),
-            sem((1,)), sem((1,)),
-            sem((7,)), sem((7,)), sem((7,)), sem((7,)),
-            sem((4,)), sem((4,)),
+            sem((2,)), sem((2,)),
+            sem((2, 7)), sem((2, 7)), sem((2, 7)), sem((2, 7)),
+            sem((2, 4)), sem((2, 4)),
         ],
         compiler_params=pltpu.CompilerParams(
             collective_id=0, has_side_effects=True, vmem_limit_bytes=48 * 2**20
@@ -478,7 +498,7 @@
         out_shape=jax.ShapeDtypeStruct((ROWS, COLS), f32),
         in_specs=[vmem, vmem],
         out_specs=vmem,
-        scratch_shapes=[square, square, square, tile, tile],
+        scratch_shapes=[square, square, square, tile, tile, pltpu.VMEM((ROWS, COLS), f32)],
         compiler_params=pltpu.CompilerParams(vmem_limit_bytes=32 * 2**20),
         name="refresh",
     )(gram, image)

time: 136 us -> 127 us (0.934)
  the two profiles are of different devices: /device:TPU:50 before, /device:TPU:10 now
where the time goes in v4:
time: 127 us
  Pallas kernels  125 us (98%)
  local copies, waits for them, and re-layouts  2.58 us (2%)
    pallas_call x1, Pallas kernels, per_device(): pl.pallas_call(gather_kernel, out_shape=(jax.ShapeDtypeStruct((ROWS, COLS...  105 us
    pallas_call x1, Pallas kernels, per_device(): pl.pallas_call(refresh_kernel, out_shape=jax.ShapeDtypeStruct((ROWS, COLS...  19.9 us
    unnamed x6, local copies, waits for them, and re-layouts  2.58 us

profile of v4, /device:TPU:10, one launch (start us, length us, event | category | flops | bytes accessed | tf_op | source)
XLA Modules:
  0.0 127.3 jit_solution(14147732809138484906)
XLA Ops:
  0.0 0.0 copy-start
  0.0 0.9 copy-done
  1.0 0.0 copy-start.1
  1.0 0.9 copy-done.1
  1.9 0.0 copy-start.2
  1.9 0.7 copy-done.2
  2.6 104.8 %gather_gram.1 = (f32[256,512]{1,0:T(8,128)S(1)}, f32[10,128,128]{2,1,0:T(8,128)S(1)}) custom-call(bf16[256,512]{1,0:T(8,128)(2,1)S(1)} %copy-done, f32[2,4]{1,0:T(2,128)S(1)} %copy-done.2, bf16[256,512]{1,0:T(8,128)(2,1)S(1)} %copy-done.1), custom_call_target="tpu_custom_call" | custom-call | tf_op jit(solution)/shard_map/gather_gram/pallas_call | solution.py:458
  107.4 19.9 %refresh.1 = f32[256,512]{1,0:T(8,128)} custom-call(f32[10,128,128]{2,1,0:T(8,128)S(1)} %get-tuple-element.7.gram_ref, f32[256,512]{1,0:T(8,128)S(1)} %get-tuple-element.8.image_ref), custom_call_target="tpu_custom_call" | custom-call | tf_op jit(solution)/shard_map/refresh/pallas_call | solution.py:496
Async XLA Ops:
  0.0 0.9 copy-start
  1.0 0.9 copy-start.1
  1.9 0.7 copy-start.2

commit v5 on v4

--- a/solution.py
+++ b/solution.py
@@ -40,7 +40,7 @@
 
 def gather_kernel(
     f_ref, scale_ref, b_ref, image_ref, gram_ref,
-    f_in, dequant, d_xy, d_yx, basis, image, image_in, part, other, mine, near, far, summed, total,
+    f_in, dequant, d_xy, d_yx, basis, image, image_in, part, other, mine, near, far, total,
     own_sem, swap_s, swap_r, xy_s, xy_r, yx_s, yx_r, ring_s, ring_r, sib_s, sib_r,
     pair_s, pair_r, rs_s, rs_r, ag_s, ag_r, across_s, across_r,
 ):
@@ -61,6 +61,9 @@
     def z_peer(d):
         return device(y, x, lax.rem(z + d, NZ), core)
 
+    def owner(d):
+        return device(y, partner_x, lax.rem(z + d, NZ), x_lo)
+
     load = pltpu.make_async_copy(f_ref, f_in, own_sem.at[4])
     load.start()
     barrier = pltpu.get_barrier_semaphore()
@@ -77,7 +80,8 @@
 
     @pl.when(moved)
     def _():
-        greet(partner)
+        for d in (0, 4, 8, 12):
+            greet(owner(d))
 
     load.wait()
     for i in range(ROWS // TILE):
@@ -87,7 +91,7 @@
 
     @pl.when(moved)
     def _():
-        pl.semaphore_wait(barrier, 15)
+        pl.semaphore_wait(barrier, 18)
 
     @pl.when(jnp.logical_not(moved))
     def _():
@@ -272,32 +276,28 @@
         for n in (1, 2, 3)
     ] for u in both]
     to_far = [[
-        remote(near[u].at[0, lax.rem(z_q + d, 4)], far[u].at[d], rs_s.at[u, 3 + d], rs_r.at[u, 3 + d], z_peer(4 * d))
+        remote(near[u].at[0, lax.rem(z_q + d, 4)], far[u].at[d], rs_s.at[u, 3 + d], rs_r.at[u, 3 + d], owner(4 * d))
         for d in (1, 2, 3)
     ] for u in both]
     for u in both:
         swap[u].wait_recv()
         mine[u][...] = part[u][core] + other[u][...]
         start(to_near[u])
+    hand = [
+        remote(near[u].at[0, z_q], far[u].at[0], swap_s.at[5 + u], swap_r.at[5 + u], partner) for u in both
+    ]
     for u in both:
         land(to_near[u])
         near[u][0] = mine[u][z_r] + near[u][1] + near[u][2] + near[u][3]
         start(to_far[u])
 
-    hand = [
-        remote(summed[u], total[u].at[core, z_r, z_q], swap_s.at[5 + u], swap_r.at[5 + u], partner) for u in both
-    ]
-    for u in both:
-        land(to_far[u])
-        summed[u][...] = near[u][0, z_q] + far[u][1] + far[u][2] + far[u][3]
-
         @pl.when(moved)
         def _(u=u):
             hand[u].start()
 
         @pl.when(jnp.logical_not(moved))
         def _(u=u):
-            total[u][core, z_r, z_q] = summed[u][...]
+            far[u][0] = near[u][0, z_q]
 
     def same(ref, send, recv, to):
         return remote(ref, ref, send, recv, to)
@@ -313,10 +313,13 @@
         for n in range(4)
     ] for u in both]
     for u in both:
+        land(to_far[u])
+
         @pl.when(moved)
         def _(u=u):
             hand[u].wait_recv()
 
+        total[u][x_lo, z_r, z_q] = far[u][0] + far[u][1] + far[u][2] + far[u][3]
         start(spread_far[u])
     for u in both:
         land(spread_far[u])
@@ -362,6 +365,12 @@
         for t in range(NZ):
             piece = total[q % PER_CORE // 3][q // PER_CORE, t % 4, t // 4, q % PER_CORE % 3]
             gram_ref[q, t * PIECE:(t + 1) * PIECE, :] = piece
+
+
+def reciprocal(value):
+    guess = pl.reciprocal(value, approx=True)
+    guess = guess * (2.0 - value * guess)
+    return guess * (2.0 - value * guess)
 
 
 def tile_inverse(s_ref, v_ref, w_ref):
@@ -387,8 +396,8 @@
             for q in range(STEP):
                 if q % 2 == 0:
                     det = block[q, q] * block[q + 1, q + 1] - block[q, q + 1] * block[q, q + 1]
-                    inv = 1.0 / block[q, q]
-                    inv_next, pivot_next = block[q, q] * (1.0 / det), det * inv
+                    inv = reciprocal(block[q, q])
+                    inv_next, pivot_next = block[q, q] * reciprocal(det), det * inv
                 else:
                     inv, block[q, q] = inv_next, pivot_next
                 pivots[g0] = jnp.where(row == r0 + q, block[q, q], pivots[g0])
@@ -477,7 +486,7 @@
             pltpu.VMEM((ROWS, COLS), f32),
             *[
                 [pltpu.VMEM((*lead, n, PIECE, TILE), f32) for _, n in SETS]
-                for lead in ((2, 4, 4), (4, 4), (4, 4), (4, 4), (4,), (), (2, 4, 4))
+                for lead in ((2, 4, 4), (4, 4), (4, 4), (4, 4), (4,), (2, 4, 4))
             ],
             sem((5,)), sem((7,)), sem((7,)),
             sem((4, 2)), sem((4, 2)), sem((4, 2)), sem((4, 2)),
@@ -487,7 +496,7 @@
             sem((2, 4)), sem((2, 4)),
         ],
         compiler_params=pltpu.CompilerParams(
-            collective_id=0, has_side_effects=True, vmem_limit_bytes=48 * 2**20
+            collective_id=0, has_side_effects=True, vmem_limit_bytes=64 * 2**20
         ),
         name="gather_gram",
     )(factor, scales, basis_block)

time: 127 us -> 129 us (1.016)
  the two profiles are of different devices: /device:TPU:10 before, /device:TPU:2 now
where the time goes in v5:
time: 129 us
  Pallas kernels  127 us (98%)
  local copies, waits for them, and re-layouts  2.12 us (2%)
    pallas_call x1, Pallas kernels, per_device(): pl.pallas_call(gather_kernel, out_shape=(jax.ShapeDtypeStruct((ROWS, COLS...  105 us
    pallas_call x1, Pallas kernels, per_device(): pl.pallas_call(refresh_kernel, out_shape=jax.ShapeDtypeStruct((ROWS, COLS...  21.8 us

profile of v5, /device:TPU:2, one launch (start us, length us, event | category | flops | bytes accessed | tf_op | source)
XLA Modules:
  0.0 128.9 jit_solution(16546136520623547577)
XLA Ops:
  0.0 104.9 %gather_gram.1 = (f32[256,512]{1,0:T(8,128)}, f32[10,128,128]{2,1,0:T(8,128)}) custom-call(bf16[256,512]{1,0:T(8,128)(2,1)} %f_ref.1, f32[2,4]{1,0:T(2,128)} %scale_ref.1, bf16[256,512]{1,0:T(8,128)(2,1)} %b_ref.1), custom_call_target="tpu_custom_call" | custom-call | tf_op jit(solution)/shard_map/gather_gram/pallas_call | solution.py:467
  104.9 0.0 copy-start
  104.9 1.1 copy-done
  106.0 0.0 copy-start.1
  106.0 1.0 copy-done.1
  107.0 21.8 %refresh.1 = f32[256,512]{1,0:T(8,128)} custom-call(f32[10,128,128]{2,1,0:T(8,128)S(1)} %copy-done, f32[256,512]{1,0:T(8,128)S(1)} %copy-done.1), custom_call_target="tpu_custom_call" | custom-call | tf_op jit(solution)/shard_map/refresh/pallas_call | solution.py:505
Async XLA Ops:
  104.9 1.1 copy-start
  106.0 1.0 copy-start.1

commit v6 on v5

--- a/solution.py
+++ b/solution.py
@@ -367,12 +367,6 @@
             gram_ref[q, t * PIECE:(t + 1) * PIECE, :] = piece
 
 
-def reciprocal(value):
-    guess = pl.reciprocal(value, approx=True)
-    guess = guess * (2.0 - value * guess)
-    return guess * (2.0 - value * guess)
-
-
 def tile_inverse(s_ref, v_ref, w_ref):
     vreg = (8, TILE)
     groups = SUB // 8
@@ -396,8 +390,8 @@
             for q in range(STEP):
                 if q % 2 == 0:
                     det = block[q, q] * block[q + 1, q + 1] - block[q, q + 1] * block[q, q + 1]
-                    inv = reciprocal(block[q, q])
-                    inv_next, pivot_next = block[q, q] * reciprocal(det), det * inv
+                    inv = 1.0 / block[q, q]
+                    inv_next, pivot_next = block[q, q] * (1.0 / det), det * inv
                 else:
                     inv, block[q, q] = inv_next, pivot_next
                 pivots[g0] = jnp.where(row == r0 + q, block[q, q], pivots[g0])
@@ -430,7 +424,12 @@
     return lax.dot_general(a, b, (over, ((), ())), precision=HIGHEST, preferred_element_type=jnp.float32)
 
 
-def refresh_kernel(gram_ref, image_ref, out_ref, a, w, v, s, vt, scaled):
+def refresh_kernel(gram_in, image_in, out_ref, gram_ref, image_ref, a, w, v, s, vt, scaled, load_sem):
+    load_gram = pltpu.make_async_copy(gram_in, gram_ref, load_sem.at[0])
+    load_image = pltpu.make_async_copy(image_in, image_ref, load_sem.at[1])
+    load_gram.start()
+    load_image.start()
+    load_gram.wait()
     eye = lax.broadcasted_iota(jnp.int32, (TILE, TILE), 0) == lax.broadcasted_iota(jnp.int32, (TILE, TILE), 1)
     down, along = [], []
     for i in range(NT):
@@ -439,6 +438,7 @@
         along.append(1.0 / jnp.sqrt(jnp.sum(diagonal, axis=0, keepdims=True)))
     for q, (i, j) in enumerate(PAIRS):
         a[i * TILE:(i + 1) * TILE, j * TILE:(j + 1) * TILE] = gram_ref[q] * (1.0 / M) * down[i] * along[j]
+    load_image.wait()
     for i in range(NT):
         scaled[:, i * TILE:(i + 1) * TILE] = image_ref[:, i * TILE:(i + 1) * TILE] * along[i]
 
@@ -505,10 +505,13 @@
     return pl.pallas_call(
         refresh_kernel,
         out_shape=jax.ShapeDtypeStruct((ROWS, COLS), f32),
-        in_specs=[vmem, vmem],
+        in_specs=[pl.BlockSpec(memory_space=pltpu.HBM)] * 2,
         out_specs=vmem,
-        scratch_shapes=[square, square, square, tile, tile, pltpu.VMEM((ROWS, COLS), f32)],
-        compiler_params=pltpu.CompilerParams(vmem_limit_bytes=32 * 2**20),
+        scratch_shapes=[
+            pltpu.VMEM((len(PAIRS), TILE, TILE), f32), pltpu.VMEM((ROWS, COLS), f32),
+            square, square, square, tile, tile, pltpu.VMEM((ROWS, COLS), f32), sem((2,)),
+        ],
+        compiler_params=pltpu.CompilerParams(vmem_limit_bytes=64 * 2**20),
         name="refresh",
     )(gram, image)
 

time: 129 us -> 126 us (0.977)
  local copies, waits for them, and re-layouts: 2.12 us -> 0 us
  Pallas kernels: 127 us -> 125 us
    unnamed x4 -> x0, local copies, waits for them, and re-layouts: 2.12 us -> none
    pallas_call x1, Pallas kernels: 21.8 us -> 20.5 us  [per_device(): pl.pallas_call(refresh_kernel, out_shape=jax.ShapeDtypeStruct((ROWS, COLS...]
where the time goes in v6:
time: 126 us
  Pallas kernels  125 us (99%)
    pallas_call x1, Pallas kernels, per_device(): pl.pallas_call(gather_kernel, out_shape=(jax.ShapeDtypeStruct((ROWS, COLS...  105 us
    pallas_call x1, Pallas kernels, per_device(): pl.pallas_call(refresh_kernel, out_shape=jax.ShapeDtypeStruct((ROWS, COLS...  20.5 us

profile of v6, /device:TPU:2, one launch (start us, length us, event | category | flops | bytes accessed | tf_op | source)
XLA Modules:
  0.0 125.6 jit_solution(6379591977164383671)
XLA Ops:
  0.0 104.9 %gather_gram.1 = (f32[256,512]{1,0:T(8,128)}, f32[10,128,128]{2,1,0:T(8,128)}) custom-call(bf16[256,512]{1,0:T(8,128)(2,1)} %f_ref.1, f32[2,4]{1,0:T(2,128)} %scale_ref.1, bf16[256,512]{1,0:T(8,128)(2,1)} %b_ref.1), custom_call_target="tpu_custom_call" | custom-call | tf_op jit(solution)/shard_map/gather_gram/pallas_call | solution.py:467
  104.9 20.5 %refresh.1 = f32[256,512]{1,0:T(8,128)} custom-call(f32[10,128,128]{2,1,0:T(8,128)} %get-tuple-element.7.gram_in, f32[256,512]{1,0:T(8,128)} %get-tuple-element.8.image_in), custom_call_target="tpu_custom_call" | custom-call | tf_op jit(solution)/shard_map/refresh/pallas_call | solution.py:505
